TPU v7x, 256 devices: a whole 4x4x8 slice. The times are simulated.
256 devices in a mesh: row: 32 (over x, y, core), col: 8 (over z).
Axes of the slice: x: 4, y: 4, z: 8, core: 2. Of those that a mesh axis runs over, the one named last changes fastest.
Arguments:
- source: bfloat16 [32768, 128], P(('row', 'col')), may hold values from -10 to 10
- target: bfloat16 [32768, 128], P(('col', 'row')), may hold values from -80 to 80
- target_potential: bfloat16 [32768], P(('col', 'row')), may hold values from -4 to 4
- prev_moment: float32 [128, 128], replicated, may hold values from -0.1 to 0.5
Outputs:
- moment: float32 [128, 128], replicated
- source_potential: float32 [32768], P('row')
- target_update: float32 [32768], P(('col', 'row'))
All inputs are finite; a program needn't handle non-finite values.
Results may differ from a plain program's by a relative error of at most 0.0059.
Values may be sent and summed in bfloat16 or wider, within the bound.
A program may use at most 64 MiB of HBM per device.

v0:
```python
import math
import jax
import jax.numpy as jnp
from jax import lax
from jax.sharding import PartitionSpec as P

ITERS = 2


def project(rows_block, matrix):
    return jnp.dot(rows_block.astype(jnp.float32), matrix, precision=lax.Precision.HIGHEST).astype(
        jnp.bfloat16
    )


def tile_costs(projected, cols_block):
    return -4.0 * lax.dot_general(
        projected, cols_block, (((1,), (1,)), ((), ())), preferred_element_type=jnp.float32
    )


def row_totals(scores):
    top_score = lax.pmax(jnp.max(scores, axis=1), "col")
    mass_total = lax.psum(jnp.sum(jnp.exp(scores - top_score[:, None]), axis=1), "col")
    return top_score + jnp.log(mass_total)


def column_totals(scores):
    top_score = lax.pmax(jnp.max(scores, axis=0), "row")
    mass_total = lax.psum(jnp.sum(jnp.exp(scores - top_score[None, :]), axis=0), "row")
    return top_score + jnp.log(mass_total)


def per_device(source, target, target_potential, prev_moment):
    rows_block = lax.all_gather(source, "col", axis=0, tiled=True)
    cols_block, potential = (
        lax.all_gather(target, "row", axis=0, tiled=True),
        lax.all_gather(target_potential, "row", axis=0, tiled=True),
    )
    row_devices = lax.axis_size("row")
    rows_total = rows_block.shape[0] * row_devices
    cols_total = cols_block.shape[0] * lax.axis_size("col")
    share_width = cols_block.shape[0] // row_devices
    position = lax.axis_index("row")
    column = potential.astype(jnp.float32)
    scores = column[None, :] - tile_costs(project(rows_block, prev_moment), cols_block)
    spread = row_totals(scores)
    weights = (jnp.exp(scores - spread[:, None]) / rows_total).astype(jnp.bfloat16)
    carried = jnp.dot(weights, cols_block, preferred_element_type=jnp.float32)
    partial_moment = lax.dot_general(
        rows_block.astype(jnp.float32),
        carried,
        (((0,), (0,)), ((), ())),
        precision=lax.Precision.HIGHEST,
    )
    moment = lax.psum(partial_moment, ("row", "col"))
    cost_tile = tile_costs(project(rows_block, moment), cols_block)
    source_potential = jnp.zeros((rows_block.shape[0],), jnp.float32)
    own_share = jnp.zeros((share_width,), jnp.float32)
    for iteration in range(ITERS):
        source_potential = math.log(cols_total) - row_totals(column[None, :] - cost_tile)
        column_scores = source_potential[:, None] - cost_tile
        column = math.log(rows_total) - column_totals(column_scores)
        own_share = lax.dynamic_slice_in_dim(column, position * share_width, share_width)
    return (moment, source_potential, own_share)


def solution(mesh):
    placed = (P(("row", "col"), None), P(("col", "row"), None), P(("col", "row")), P())
    return jax.shard_map(
        per_device,
        mesh=mesh,
        in_specs=placed,
        out_specs=(P(), P("row"), P(("col", "row"))),
        check_vma=False,
    )
```

profile of v0, /device:TPU:32, one launch (start us, length us, event | category | flops | bytes accessed | tf_op | source)
XLA Modules:
  0.0 979.2 jit_solution(412638877074749381)
XLA Ops:
  7.2 0.7 all-gather.3.cloned.1.call-update
  7.9 0.0 all-reduce.2.cloned.1.call-start
  8.0 21.8 %all-gather = bf16[32,1,128]{2,1,0:T(2,128)(2,1)S(1)} all-gather(bf16[1,1,128]{2,1,0:T(2,128)(2,1)} %bitcast.20), channel_id=1, replica_groups=mesh['row'=32,'col'=8] {'row'}, dimensions={0}, use_global_device_ids=true | all-gather | bytes 8448 | tf_op jit(solution)/shard_map/all_gather | solution.py:38
  29.8 27.7 %all_gather.10 = bf16[1024,128]{1,0:T(8,128)(2,1)S(1)} all-gather(bf16[128,128]{1,0:T(8,128)(2,1)} %param.4), channel_id=1, replica_groups=mesh['row'=32,'col'=8] {'col'}, dimensions={0}, use_global_device_ids=true | all-gather | bytes 294912 | tf_op jit(solution)/shard_map/all_gather | solution.py:35
  57.5 0.4 convolution_convert_fusion.1
  57.9 3.1 all-gather.3.cloned.1.call-done
  61.0 8.3 fusion
  69.3 16.0 %pmax.35 = f32[1024]{0:T(1024)S(1)} all-reduce(f32[1024]{0:T(1024)S(1)} %get-tuple-element.9), channel_id=1, replica_groups=mesh['row'=32,'col'=8] {'col'}, use_global_device_ids=true, to_apply=%region_1.0 | all-reduce | flops 1024 | bytes 8192 | tf_op jit(solution)/shard_map/pmax | solution.py:23
  85.4 7.8 exponential_reduce_fusion.4
  93.2 16.0 %psum.42 = f32[1024]{0:T(1024)S(1)} all-reduce(f32[1024]{0:T(1024)S(1)} %exponential_reduce_fusion.4), channel_id=1, replica_groups=mesh['row'=32,'col'=8] {'col'}, use_global_device_ids=true, to_apply=%region_3.0 | all-reduce | flops 1024 | bytes 8192 | tf_op jit(solution)/shard_map/psum | solution.py:24
  109.2 7.8 fusion.1
  117.0 1.2 convolution_bitcast_fusion
  118.3 234.4 %all-reduce.2.cloned.1.call-done = f32[128,128]{0,1:T(8,128)} async-done(((f32[128,128]{0,1:T(8,128)}), f32[128,128]{0,1:T(8,128)}) %all-reduce.2.cloned.1.call-update) | async-done | bytes 65552 | tf_op jit(solution)/shard_map/psum | solution.py:56
  352.7 1.2 convolution_convert_fusion
  353.9 7.0 subtract_reduce_fusion.3
  360.9 15.2 %pmax.36 = f32[1024]{0:T(1024)S(1)} all-reduce(f32[1024]{0:T(1024)S(1)} %get-tuple-element.11), channel_id=1, replica_groups=mesh['row'=32,'col'=8] {'col'}, use_global_device_ids=true, to_apply=%region_6.0 | all-reduce | flops 1024 | bytes 8192 | tf_op jit(solution)/shard_map/pmax | solution.py:23
  376.1 7.8 exponential_reduce_fusion.3
  384.0 15.1 %psum.44 = f32[1024]{0:T(1024)S(1)} all-reduce(f32[1024]{0:T(1024)S(1)} %exponential_reduce_fusion.3), channel_id=1, replica_groups=mesh['row'=32,'col'=8] {'col'}, use_global_device_ids=true, to_apply=%region_8.0 | all-reduce | flops 1024 | bytes 8192 | tf_op jit(solution)/shard_map/psum | solution.py:24
  399.1 7.7 subtract_reduce_fusion.2
  406.8 124.0 %pmax.37 = f32[4096]{0:T(1024)S(1)} all-reduce(f32[4096]{0:T(1024)S(1)} %subtract_reduce_fusion.2), channel_id=1, replica_groups=mesh['row'=32,'col'=8] {'row'}, use_global_device_ids=true, to_apply=%region_10.0 | all-reduce | flops 4096 | bytes 32768 | tf_op jit(solution)/shard_map/pmax | solution.py:29
  530.8 7.7 exponential_reduce_fusion.2
  538.5 123.8 %psum.45 = f32[4096]{0:T(1024)S(1)} all-reduce(f32[4096]{0:T(1024)S(1)} %exponential_reduce_fusion.2), channel_id=1, replica_groups=mesh['row'=32,'col'=8] {'row'}, use_global_device_ids=true, to_apply=%region_12.0 | all-reduce | flops 4096 | bytes 32768 | tf_op jit(solution)/shard_map/psum | solution.py:30
  662.3 7.5 subtract_reduce_fusion.1
  669.8 15.2 %pmax.38 = f32[1024]{0:T(1024)S(1)} all-reduce(f32[1024]{0:T(1024)S(1)} %subtract_reduce_fusion.1), channel_id=1, replica_groups=mesh['row'=32,'col'=8] {'col'}, use_global_device_ids=true, to_apply=%region_14.0 | all-reduce | flops 1024 | bytes 8192 | tf_op jit(solution)/shard_map/pmax | solution.py:23
  685.0 7.8 exponential_reduce_fusion.1
  692.8 15.1 %psum.46 = f32[1024]{0:T(1024)S(1)} all-reduce(f32[1024]{0:T(1024)S(1)} %exponential_reduce_fusion.1), channel_id=1, replica_groups=mesh['row'=32,'col'=8] {'col'}, use_global_device_ids=true, to_apply=%region_16.0 | all-reduce | flops 1024 | bytes 8192 | tf_op jit(solution)/shard_map/psum | solution.py:24
  708.0 7.8 subtract_reduce_fusion
  715.7 123.8 %pmax.39 = f32[4096]{0:T(1024)S(1)} all-reduce(f32[4096]{0:T(1024)S(1)} %subtract_reduce_fusion), channel_id=1, replica_groups=mesh['row'=32,'col'=8] {'row'}, use_global_device_ids=true, to_apply=%region_18.0 | all-reduce | flops 4096 | bytes 32768 | tf_op jit(solution)/shard_map/pmax | solution.py:29
  839.5 7.7 exponential_reduce_fusion
  847.3 123.8 %psum.47 = f32[4096]{0:T(1024)S(1)} all-reduce(f32[4096]{0:T(1024)S(1)} %exponential_reduce_fusion), channel_id=1, replica_groups=mesh['row'=32,'col'=8] {'row'}, use_global_device_ids=true, to_apply=%region_20.0 | all-reduce | flops 4096 | bytes 32768 | tf_op jit(solution)/shard_map/psum | solution.py:30
  971.0 0.6 fusion.2
  971.6 0.7 copy.8
  (15 shorter events, 0.1 us)
Async XLA Ops:
  7.2 50.3 %copy-start = (f32[128,128]{1,0:T(8,128)S(1)}, f32[128,128]{1,0:T(8,128)}, u32[]{:S(2)}) copy-start(f32[128,128]{1,0:T(8,128)} %param.7) | copy-start | bytes 196612
  7.2 53.8 %all-gather.3.cloned.1.call-start = ((), (), s32[]{:S(2)}) async-start(), calls=%async_computation | async-start | bytes 1081344 | tf_op jit(solution)/shard_map/all_gather | solution.py:37
  7.9 344.7 %all-reduce.2.cloned.1.call-start = ((), (), s32[]{:S(2)}) async-start(), calls=%async_computation.1 | async-start | bytes 131072 | tf_op jit(solution)/shard_map/psum | solution.py:56
  61.0 48.2 %copy-start.1 = (bf16[4096,128]{1,0:T(8,128)(2,1)S(1)}, bf16[4096,128]{1,0:T(8,128)(2,1)}, u32[]{:S(2)}) copy-start(bf16[4096,128]{1,0:T(8,128)(2,1)} %all-gather.3.cloned.1.call-done) | copy-start | bytes 3145732
  708.0 139.3 %copy-start.3 = (f32[1024]{0:T(1024)}, f32[1024]{0:T(1024)S(1)}, u32[]{:S(2)}) copy-start(f32[1024]{0:T(1024)S(1)} %add_subtract_fusion.1) | copy-start | bytes 12292
  708.0 263.7 %copy-start.2 = (f32[128,128]{0,1:T(8,128)S(1)}, f32[128,128]{0,1:T(8,128)}, u32[]{:S(2)}) copy-start(f32[128,128]{0,1:T(8,128)} %all-reduce.2.cloned.1.call-done) | copy-start | bytes 196612
Sparse Core Ops, SparseCore 0:
  10.6 50.3 all-gather.2
  118.4 234.2 all-reduce.1
where the time goes:
time: 980 us; the launch traced here: 979 us
  blocking collectives  638 us (65%)
  waiting for transfers between devices  238 us (24%)
  other arithmetic  62.6 us (6%)
  matrix products  25.9 us (3%)
  between operations  14.1 us (1%)
    pmax x2, blocking collectives, column_totals(): top_score = lax.pmax(jnp.max(scores, axis=0), 'row')  248 us
    psum x2, blocking collectives, column_totals(): lax.psum(jnp.sum(jnp.exp(scores - top_score[None, :]), axis=0), 'row')  248 us
    psum x1, waiting for transfers between devices, per_device(): moment = lax.psum(partial_moment, ('row', 'col'))  234 us
    pmax x3, blocking collectives, row_totals(): top_score = lax.pmax(jnp.max(scores, axis=1), 'col')  46.5 us
    psum x3, blocking collectives, row_totals(): lax.psum(jnp.sum(jnp.exp(scores - top_score[:, None]), axis=1), 'col')  46.2 us
    all_gather x1, blocking collectives, per_device(): rows_block = lax.all_gather(source, 'col', axis=0, tiled=True)  27.7 us
    reduce_sum x3, other arithmetic, row_totals(): jnp.sum(jnp.exp(scores - top_score[:, None]), axis=1)  23.5 us
    all_gather x1, blocking collectives, per_device(): lax.all_gather(target_potential, 'row', axis=0, tiled=True)  21.8 us
  transfers between devices with their start and end apart: 2, of which 2 were waited for; matrix products, arithmetic and copies ran while one was open for 0% of the time, Pallas kernels for 0%

commit v1 on v0

--- a/solution.py
+++ b/solution.py
@@ -53,7 +53,7 @@
         (((0,), (0,)), ((), ())),
         precision=lax.Precision.HIGHEST,
     )
-    moment = lax.psum(partial_moment, ("row", "col"))
+    moment = lax.psum(lax.psum(partial_moment, "col"), "row")
     cost_tile = tile_costs(project(rows_block, moment), cols_block)
     source_potential = jnp.zeros((rows_block.shape[0],), jnp.float32)
     own_share = jnp.zeros((share_width,), jnp.float32)

time: 980 us -> 924 us (0.943)
  waiting for transfers between devices: 238 us -> 181 us
    psum x1 -> x2, waiting for transfers between devices: 234 us -> 177 us  [per_device(): moment = lax.psum(lax.psum(partial_moment, 'col'), 'row')]
  transfers between devices with their start and end apart: 2 -> 3, of which waited for: 2 -> 3; matrix products, arithmetic and copies ran while one was open for 0% -> 0% of each run, Pallas kernels for 0% -> 0%
where the time goes in v1:
time: 924 us; the launch traced here: 923 us
  blocking collectives  639 us (69%)
  waiting for transfers between devices  181 us (20%)
  other arithmetic  62.6 us (7%)
  matrix products  25.9 us (3%)
  between operations  13.8 us (1%)
    pmax x2, blocking collectives, column_totals(): top_score = lax.pmax(jnp.max(scores, axis=0), 'row')  248 us
    psum x2, blocking collectives, column_totals(): lax.psum(jnp.sum(jnp.exp(scores - top_score[None, :]), axis=0), 'row')  248 us
    psum x2, waiting for transfers between devices, per_device(): moment = lax.psum(lax.psum(partial_moment, 'col'), 'row')  177 us
    psum x3, blocking collectives, row_totals(): lax.psum(jnp.sum(jnp.exp(scores - top_score[:, None]), axis=1), 'col')  47.3 us
    pmax x3, blocking collectives, row_totals(): top_score = lax.pmax(jnp.max(scores, axis=1), 'col')  47.1 us
    all_gather x1, blocking collectives, per_device(): rows_block = lax.all_gather(source, 'col', axis=0, tiled=True)  27.7 us
    reduce_sum x3, other arithmetic, row_totals(): jnp.sum(jnp.exp(scores - top_score[:, None]), axis=1)  23.5 us
    all_gather x1, blocking collectives, per_device(): lax.all_gather(target_potential, 'row', axis=0, tiled=True)  21.8 us
  transfers between devices with their start and end apart: 3, of which 3 were waited for; matrix products, arithmetic and copies ran while one was open for 0% of the time, Pallas kernels for 0%

profile of v1, /device:TPU:32, one launch (start us, length us, event | category | flops | bytes accessed | tf_op | source)
XLA Modules:
  0.0 923.3 jit_solution(5181491558607512836)
XLA Ops:
  7.2 0.7 all-gather.3.cloned.1.call-update
  8.0 21.8 %all-gather = bf16[32,1,128]{2,1,0:T(2,128)(2,1)S(1)} all-gather(bf16[1,1,128]{2,1,0:T(2,128)(2,1)} %bitcast.20), channel_id=1, replica_groups=mesh['row'=32,'col'=8] {'row'}, dimensions={0}, use_global_device_ids=true | all-gather | bytes 8448 | tf_op jit(solution)/shard_map/all_gather | solution.py:38
  29.8 27.7 %all_gather.10 = bf16[1024,128]{1,0:T(8,128)(2,1)S(1)} all-gather(bf16[128,128]{1,0:T(8,128)(2,1)} %param.4), channel_id=1, replica_groups=mesh['row'=32,'col'=8] {'col'}, dimensions={0}, use_global_device_ids=true | all-gather | bytes 294912 | tf_op jit(solution)/shard_map/all_gather | solution.py:35
  57.5 0.4 convolution_convert_fusion.1
  57.9 3.1 all-gather.3.cloned.1.call-done
  61.0 8.3 fusion
  69.3 16.0 %pmax.35 = f32[1024]{0:T(1024)S(1)} all-reduce(f32[1024]{0:T(1024)S(1)} %get-tuple-element.9), channel_id=1, replica_groups=mesh['row'=32,'col'=8] {'col'}, use_global_device_ids=true, to_apply=%region_1.0 | all-reduce | flops 1024 | bytes 8192 | tf_op jit(solution)/shard_map/pmax | solution.py:23
  85.4 7.8 exponential_reduce_fusion.4
  93.2 16.0 %psum.49 = f32[1024]{0:T(1024)S(1)} all-reduce(f32[1024]{0:T(1024)S(1)} %exponential_reduce_fusion.4), channel_id=1, replica_groups=mesh['row'=32,'col'=8] {'col'}, use_global_device_ids=true, to_apply=%region_3.0 | all-reduce | flops 1024 | bytes 8192 | tf_op jit(solution)/shard_map/psum | solution.py:24
  109.2 7.8 fusion.1
  117.0 1.2 convolution_bitcast_fusion
  118.3 68.9 %all-reduce.3.cloned.1.call-done = f32[128,128]{0,1:T(8,128)} async-done(((f32[128,128]{0,1:T(8,128)}), f32[128,128]{0,1:T(8,128)}) %all-reduce.3.cloned.1.call-update) | async-done | bytes 65552 | tf_op jit(solution)/shard_map/psum | solution.py:56
  187.2 108.0 %all-reduce.5.cloned.1.call-done = f32[128,128]{0,1:T(8,128)} async-done(((f32[128,128]{0,1:T(8,128)}), f32[128,128]{0,1:T(8,128)}) %all-reduce.5.cloned.1.call-update) | async-done | bytes 65552 | tf_op jit(solution)/shard_map/psum | solution.py:56
  295.3 1.2 convolution_convert_fusion
  296.5 7.0 subtract_reduce_fusion.3
  303.5 16.1 %pmax.36 = f32[1024]{0:T(1024)S(1)} all-reduce(f32[1024]{0:T(1024)S(1)} %get-tuple-element.11), channel_id=1, replica_groups=mesh['row'=32,'col'=8] {'col'}, use_global_device_ids=true, to_apply=%region_7.0 | all-reduce | flops 1024 | bytes 8192 | tf_op jit(solution)/shard_map/pmax | solution.py:23
  319.6 7.8 exponential_reduce_fusion.3
  327.4 16.0 %psum.52 = f32[1024]{0:T(1024)S(1)} all-reduce(f32[1024]{0:T(1024)S(1)} %exponential_reduce_fusion.3), channel_id=1, replica_groups=mesh['row'=32,'col'=8] {'col'}, use_global_device_ids=true, to_apply=%region_9.0 | all-reduce | flops 1024 | bytes 8192 | tf_op jit(solution)/shard_map/psum | solution.py:24
  343.4 7.7 subtract_reduce_fusion.2
  351.2 124.0 %pmax.37 = f32[4096]{0:T(1024)S(1)} all-reduce(f32[4096]{0:T(1024)S(1)} %subtract_reduce_fusion.2), channel_id=1, replica_groups=mesh['row'=32,'col'=8] {'row'}, use_global_device_ids=true, to_apply=%region_11.0 | all-reduce | flops 4096 | bytes 32768 | tf_op jit(solution)/shard_map/pmax | solution.py:29
  475.1 7.7 exponential_reduce_fusion.2
  482.9 123.8 %psum.53 = f32[4096]{0:T(1024)S(1)} all-reduce(f32[4096]{0:T(1024)S(1)} %exponential_reduce_fusion.2), channel_id=1, replica_groups=mesh['row'=32,'col'=8] {'row'}, use_global_device_ids=true, to_apply=%region_13.0 | all-reduce | flops 4096 | bytes 32768 | tf_op jit(solution)/shard_map/psum | solution.py:30
  606.7 7.5 subtract_reduce_fusion.1
  614.1 15.0 %pmax.38 = f32[1024]{0:T(1024)S(1)} all-reduce(f32[1024]{0:T(1024)S(1)} %subtract_reduce_fusion.1), channel_id=1, replica_groups=mesh['row'=32,'col'=8] {'col'}, use_global_device_ids=true, to_apply=%region_15.0 | all-reduce | flops 1024 | bytes 8192 | tf_op jit(solution)/shard_map/pmax | solution.py:23
  629.2 7.8 exponential_reduce_fusion.1
  637.0 15.3 %psum.54 = f32[1024]{0:T(1024)S(1)} all-reduce(f32[1024]{0:T(1024)S(1)} %exponential_reduce_fusion.1), channel_id=1, replica_groups=mesh['row'=32,'col'=8] {'col'}, use_global_device_ids=true, to_apply=%region_17.0 | all-reduce | flops 1024 | bytes 8192 | tf_op jit(solution)/shard_map/psum | solution.py:24
  652.3 7.8 subtract_reduce_fusion
  660.1 123.8 %pmax.39 = f32[4096]{0:T(1024)S(1)} all-reduce(f32[4096]{0:T(1024)S(1)} %subtract_reduce_fusion), channel_id=1, replica_groups=mesh['row'=32,'col'=8] {'row'}, use_global_device_ids=true, to_apply=%region_19.0 | all-reduce | flops 4096 | bytes 32768 | tf_op jit(solution)/shard_map/pmax | solution.py:29
  783.9 7.7 exponential_reduce_fusion
  791.6 123.8 %psum.55 = f32[4096]{0:T(1024)S(1)} all-reduce(f32[4096]{0:T(1024)S(1)} %exponential_reduce_fusion), channel_id=1, replica_groups=mesh['row'=32,'col'=8] {'row'}, use_global_device_ids=true, to_apply=%region_21.0 | all-reduce | flops 4096 | bytes 32768 | tf_op jit(solution)/shard_map/psum | solution.py:30
  915.4 0.6 fusion.2
  916.0 0.7 copy.8
  (18 shorter events, 0.2 us)
Async XLA Ops:
  7.2 50.3 %copy-start = (f32[128,128]{1,0:T(8,128)S(1)}, f32[128,128]{1,0:T(8,128)}, u32[]{:S(2)}) copy-start(f32[128,128]{1,0:T(8,128)} %param.7) | copy-start | bytes 196612
  7.2 53.8 %all-gather.3.cloned.1.call-start = ((), (), s32[]{:S(2)}) async-start(), calls=%async_computation | async-start | bytes 1081344 | tf_op jit(solution)/shard_map/all_gather | solution.py:37
  7.9 179.3 %all-reduce.3.cloned.1.call-start = ((), (), s32[]{:S(2)}) async-start(), calls=%async_computation.1 | async-start | bytes 131072 | tf_op jit(solution)/shard_map/psum | solution.py:56
  61.0 48.2 %copy-start.1 = (bf16[4096,128]{1,0:T(8,128)(2,1)S(1)}, bf16[4096,128]{1,0:T(8,128)(2,1)}, u32[]{:S(2)}) copy-start(bf16[4096,128]{1,0:T(8,128)(2,1)} %all-gather.3.cloned.1.call-done) | copy-start | bytes 3145732
  118.3 177.0 %all-reduce.5.cloned.1.call-start = ((), (), s32[]{:S(2)}) async-start(), calls=%async_computation.2 | async-start | bytes 131072 | tf_op jit(solution)/shard_map/psum | solution.py:56
  652.3 139.3 %copy-start.3 = (f32[1024]{0:T(1024)}, f32[1024]{0:T(1024)S(1)}, u32[]{:S(2)}) copy-start(f32[1024]{0:T(1024)S(1)} %add_subtract_fusion.1) | copy-start | bytes 12292
  652.3 263.7 %copy-start.2 = (f32[128,128]{0,1:T(8,128)S(1)}, f32[128,128]{0,1:T(8,128)}, u32[]{:S(2)}) copy-start(f32[128,128]{0,1:T(8,128)} %all-reduce.5.cloned.1.call-done) | copy-start | bytes 196612
Sparse Core Ops, SparseCore 0:
  10.6 50.3 all-gather.2
  118.4 68.7 all-reduce.2
  190.8 104.4 all-reduce.4
